TPU v7x, 256 devices: a whole 4x4x8 slice. The times are simulated.
256 devices in a mesh: inputs: 64 (over x_hi, y, z), tm: 4 (over x_lo, core).
Axes of the slice: x: 4 (x_hi: 2, x_lo: 2; x = x_hi * 2 + x_lo), y: 4, z: 8, core: 2. Of those that a mesh axis runs over, the one named last changes fastest.
Arguments:
- voltages: bfloat16 [1024, 131072], P('inputs', 'tm'), may hold values from -8 to 8
- pfb_taps: float32 [8, 512], replicated, may hold values from -2 to 2
Outputs:
- visibilities: float32 [256, 36, 2, 128, 128], P(('inputs', 'tm'))
All inputs are finite; a program needn't handle non-finite values.
Results may differ from a plain program's by a relative error of at most 0.002.
Values may be sent and summed in bfloat16 or wider, within the bound.
A program may use at most 128 MiB of HBM per device.

v0:
```python
import jax
import jax.numpy as jnp
from jax import lax
from jax.sharding import PartitionSpec as P

F = 256
TAPS = 8
TILE = 128
FRAME = 512


def from_behind(value, axis, steps):
    count = lax.axis_size(axis)
    initial, last = (max(0, -steps), min(count, count - steps))
    return lax.ppermute(value, axis, [(source, source + steps) for source in range(initial, last)])


def dft_table(chans, length):
    rows = jnp.arange(2 * chans, dtype=jnp.int32)
    freq = rows // 2
    part = rows % 2
    samp = jnp.arange(length, dtype=jnp.int32)
    phase = freq[:, None] * samp[None, :] % length
    angle = 2.0 * jnp.pi / length * phase.astype(jnp.float32)
    vals = jnp.where(part[:, None] == 0, jnp.cos(angle), -jnp.sin(angle))
    return (vals * (1.0 / length**0.5)).astype(jnp.bfloat16)


def tile_sums(spec, scale):
    left = jnp.concatenate([spec[:, 0], spec[:, 1]], axis=-1)
    twisted = jnp.concatenate([spec[:, 1], -spec[:, 0]], axis=-1)
    count_in = left.shape[1]
    blocks = count_in // TILE
    chans = left.shape[0]
    real_rows = []
    imag_rows = []
    for first in range(blocks):
        lower = first * TILE
        cols = left[:, lower:]
        real_part = jnp.einsum(
            "cik,cjk->cij", left[:, lower : lower + TILE], cols, preferred_element_type=jnp.float32
        )
        imag_part = jnp.einsum(
            "cik,cjk->cij",
            twisted[:, lower : lower + TILE],
            cols,
            preferred_element_type=jnp.float32,
        )
        count = blocks - first
        real_rows.append(real_part.reshape(chans, TILE, count, TILE).transpose(0, 2, 1, 3))
        imag_rows.append(imag_part.reshape(chans, TILE, count, TILE).transpose(0, 2, 1, 3))
    real_all = jnp.concatenate(real_rows, axis=1)
    imag_all = jnp.concatenate(imag_rows, axis=1)
    return jnp.stack([real_all, imag_all], axis=2) * scale


def on_device(voltages, pfb_taps):
    inp_local = voltages.shape[0]
    frames_local = voltages.shape[1] // FRAME
    previous = from_behind(voltages[:, voltages.shape[1] - (TAPS - 1) * FRAME :], "tm", 1)
    extended = jnp.concatenate([previous, voltages], axis=1).reshape(
        inp_local, frames_local + TAPS - 1, FRAME
    )
    filtered = jnp.zeros((inp_local, frames_local, FRAME), jnp.float32)
    for tap in range(TAPS):
        filtered = filtered + pfb_taps[tap][None, None, :] * extended[
            :, tap : tap + frames_local, :
        ].astype(jnp.float32)
    filtered = filtered.astype(jnp.bfloat16)
    table = dft_table(F, FRAME)
    spectra = jnp.einsum("kn,itn->kit", table, filtered, preferred_element_type=jnp.float32)
    spectra = spectra.astype(jnp.bfloat16).reshape(F, 2, inp_local, frames_local)
    blocks_time = lax.axis_size("tm")
    scale = 1.0 / (frames_local * blocks_time)
    turned = lax.all_to_all(spectra, "inputs", split_axis=0, concat_axis=2, tiled=True)
    return lax.psum_scatter(tile_sums(turned, scale), "tm", scatter_dimension=0, tiled=True)


def solution(mesh):
    in_specs = (P("inputs", "tm"), P())
    out_specs = P(("inputs", "tm"), None, None, None, None)
    return jax.shard_map(
        on_device, mesh=mesh, in_specs=in_specs, out_specs=out_specs, check_vma=False
    )
```

profile of v0, /device:TPU:1, one launch (start us, length us, event | category | flops | bytes accessed | tf_op | source)
XLA Modules:
  0.0 323.3 jit_solution(11821834543448941086)
XLA Ops:
  6.5 0.9 slice.127
  7.4 4.5 %collective-permute-start = (bf16[16,3584]{1,0:T(8,128)(2,1)S(1)}, bf16[16,3584]{1,0:T(8,128)(2,1)S(1)}, u32[]{:S(2)}, u32[]{:S(2)}) collective-permute-start(bf16[16,3584]{1,0:T(8,128)(2,1)S(1)} %slice.127), channel_id=1, source_target_pairs={{0,1},{1,2},{2,3},{4,5},{5,6},{6,7},{8,9},{9,10},{10,11},{12,13},{... | collective-permute-start | bytes 344072 | tf_op jit(solution)/shard_map/ppermute | solution.py:15
  11.9 1.0 fusion.121
  13.7 1.3 pad_maximum_fusion
  15.7 6.5 %convolution_convert_fusion = bf16[512,16,64]{0,2,1:T(8,128)(2,1)S(1)} fusion(bf16[16,71,512]{2,1,0:T(8,128)(2,1)S(1)} %reshape.80, f32[512]{0:T(512)S(1)} %bitcast.140, f32[512]{0:T(512)S(1)} %bitcast.141, f32[512]{0:T(512)S(1)} %bitcast.135, f32[512]{0:T(512)S(1)} %bitcast.136, f32[512]{0:T(512)S(1)} %bitcast.137, f32[512]{0:T(512)S(1)} %bitcast.138, ...), kind=kOutput, calls=%fused_computation.11 | convolution fusion | flops 554696704 | bytes 9456128 | tf_op jit(solution)/shard_map/kn,itn->kit/dot_general | solution.py:71
  22.3 2.0 copy.20
  24.3 1.5 reshape.97
  25.8 42.6 %all_to_all.18 = bf16[64,2,4096]{2,1,0:T(2,128)(2,1)} all-to-all(bf16[64,2,4096]{2,1,0:T(2,128)(2,1)S(1)} %reshape.97), channel_id=1, replica_groups=mesh['inputs'=64,'tm'=4] {'inputs'}, dimensions={0} | all-to-all | bytes 2097152 | tf_op jit(solution)/shard_map/all_to_all | solution.py:75
  68.4 3.8 %reshape.98 = bf16[256,2,16,64]{3,2,1,0:T(8,128)(2,1)S(1)} reshape(bf16[64,2,4096]{2,1,0:T(2,128)(2,1)} %all_to_all.18) | data formatting | bytes 2097152
  73.5 1.9 fusion.26
  75.4 1.8 fusion.59
  77.2 1.6 fusion.55
  78.8 1.5 convolution_bitcast_fusion.3
  80.3 1.3 fusion.48
  81.6 1.1 convolution_bitcast_fusion.5
  82.8 1.8 fusion.37
  84.6 1.9 fusion.25
  86.6 2.1 convolution_bitcast_fusion
  88.6 1.6 fusion.39
  90.3 1.5 convolution_bitcast_fusion.2
  91.8 1.3 fusion.42
  93.0 1.1 convolution_bitcast_fusion.4
  94.2 1.6 fusion.1
  95.8 2.8 copy.29
  98.5 3.0 copy.30
  101.5 2.8 copy.31
  104.4 2.3 copy.32
  106.7 3.0 constant_dynamic-update-slice_fusion.3
  109.7 1.4 constant_dynamic-update-slice_fusion.2
  111.6 1.2 constant_dynamic-update-slice_fusion.1
  113.3 1.1 fusion.8
  114.4 1.0 constant_dynamic-update-slice_fusion
  115.4 0.9 fusion.15
  116.2 1.0 fusion.3
  117.2 3.0 copy.42
  120.2 2.7 copy.41
  123.0 3.2 fusion
  126.2 2.8 copy.43
  129.0 2.3 copy.44
  131.3 3.1 constant_dynamic-update-slice_fusion.7
  134.3 1.4 constant_dynamic-update-slice_fusion.6
  136.2 1.2 constant_dynamic-update-slice_fusion.5
  137.9 1.1 fusion.7
  139.0 1.0 constant_dynamic-update-slice_fusion.4
  140.0 0.8 fusion.14
  140.8 1.0 fusion.2
  141.8 13.3 %maximum_multiply_fusion = f32[4,36,2,128,128]{4,3,2,1,0:T(8,128)} fusion(f32[4,36,1,128,128]{4,3,2,1,0:T(8,128)} %bitcast.121, f32[4,36,1,128,128]{4,3,2,1,0:T(8,128)} %bitcast.120), kind=kLoop, calls=%fused_computation | loop fusion | flops 9437184 | bytes 37748736 | tf_op jit(solution)/shard_map/mul | solution.py:54
  155.1 161.4 %reduce-scatter.2.cloned.1.call-done = f32[1,36,2,128,128]{4,3,2,1,0:T(8,128)} async-done(((f32[4,36,2,128,128]{4,3,2,1,0:T(8,128)}), f32[1,36,2,128,128]{4,3,2,1,0:T(8,128)}) %reduce-scatter.2.cloned.1.call-update) | async-done | bytes 4718608 | tf_op jit(solution)/shard_map/reduce_scatter | solution.py:76
  (30 shorter events, 4.9 us)
Async XLA Ops:
  6.5 310.0 %reduce-scatter.2.cloned.1.call-start = ((), (), s32[]{:S(2)}) async-start(), calls=%async_computation.2 | async-start | bytes 23592960 | tf_op jit(solution)/shard_map/reduce_scatter | solution.py:76
  7.4 6.3 %collective-permute-start = (bf16[16,3584]{1,0:T(8,128)(2,1)S(1)}, bf16[16,3584]{1,0:T(8,128)(2,1)S(1)}, u32[]{:S(2)}, u32[]{:S(2)}) collective-permute-start(bf16[16,3584]{1,0:T(8,128)(2,1)S(1)} %slice.127), channel_id=1, source_target_pairs={{0,1},{1,2},{2,3},{4,5},{5,6},{6,7},{8,9},{9,10},{10,11},{12,13},{... | collective-permute-start | bytes 344072 | tf_op jit(solution)/shard_map/ppermute | solution.py:15
  106.7 3.0 copy-start.1
  109.7 1.9 copy-start.2
  111.6 1.7 copy-start.5
  111.6 2.8 copy-start.6
  113.3 2.1 copy-start.9
  131.3 3.1 copy-start
  134.3 1.9 copy-start.3
  136.2 1.7 copy-start.4
  136.2 2.8 copy-start.7
  137.9 2.1 copy-start.8
Sparse Core Ops, SparseCore 0:
  155.2 161.2 reduce-scatter.1
where the time goes:
time: 324 us; the launch traced here: 323 us
  waiting for transfers between devices  162 us (50%)
  local copies, waits for them, and re-layouts  56.1 us (17%)
  blocking collectives  42.6 us (13%)
  matrix products  29.9 us (9%)
  other arithmetic  14.7 us (5%)
  between operations  13.5 us (4%)
  starting transfers between devices  4.5 us (1%)
    reduce_scatter x1, waiting for transfers between devices, on_device(): lax.psum_scatter(tile_sums(turned, scale), 'tm', scatter_dimension=0, til...  161 us
    all_to_all x1, blocking collectives, on_device(): lax.all_to_all(spectra, 'inputs', split_axis=0, concat_axis=2, tiled=True)  42.6 us
    unnamed x36, local copies, waits for them, and re-layouts  29.1 us
    mul x1, other arithmetic, tile_sums(): return jnp.stack([real_all, imag_all], axis=2) * scale  13.3 us
    dot_general x8, matrix products, tile_sums(): jnp.einsum('cik,cjk->cij', twisted[:, lower:lower + TILE], cols, preferre...  12.4 us
    dot_general x8, matrix products, tile_sums(): jnp.einsum('cik,cjk->cij', left[:, lower:lower + TILE], cols, preferred_e...  10.9 us
    transpose x4, local copies, waits for them, and re-layouts, tile_sums(): real_part.reshape(chans, TILE, count, TILE).transpose(0, 2, 1, 3)  10.9 us
    transpose x4, local copies, waits for them, and re-layouts, tile_sums(): imag_part.reshape(chans, TILE, count, TILE).transpose(0, 2, 1, 3)  10.9 us
  transfers between devices with their start and end apart: 2, of which 2 were waited for; matrix products, arithmetic and copies ran while one was open for 0% of the time, Pallas kernels for 0%

commit v1 on v0

v1 whole, which is shorter than its diff:
```python
import functools

import jax
import jax.numpy as jnp
import numpy as np
from jax import lax
from jax.experimental import pallas as pl
from jax.experimental.pallas import tpu as pltpu
from jax.sharding import PartitionSpec as P

F = 256
TAPS = 8
TILE = 128
FRAME = 512
HALO = (TAPS - 1) * FRAME
LANES = 128
MESH = pl.DeviceIdType.MESH


def dft_table(chans, length, owners):
    freq = np.arange(chans, dtype=np.int32)
    samp = np.arange(length, dtype=np.int32)
    phase = (freq[:, None] * samp[None, :]) % length
    angle = 2.0 * np.pi / length * phase.astype(np.float64)
    vals = np.stack([np.cos(angle), -np.sin(angle)]) / length**0.5
    vals = vals.reshape(2, chans // owners, owners, length).transpose(2, 0, 1, 3)
    return vals.reshape(2 * chans, length).astype(np.float32).astype(jnp.bfloat16)


def grid_coords():
    along = lax.axis_index("inputs")
    block = lax.axis_index("tm")
    return along // 32, (along // 8) % 4, along % 8, block


def grid_device(x_hi, y, z, block):
    return (x_hi * 32 + y * 8 + z, block)


def channel_kernel(
    frames, v_hbm, taps_ref, table_hbm, recv,
    volts, table, halo, filt32, filt, stage, send,
    in_sems, halo_send, halo_recv, send_sem, recv_sem, y_sem, x_sem,
):
    x_hi, y, z, block = grid_coords()
    blocks = 4
    groups = 64
    inp = v_hbm.shape[0]

    load_volts = pltpu.make_async_copy(v_hbm, volts, in_sems.at[0])
    load_table = pltpu.make_async_copy(table_hbm, table, in_sems.at[1])
    load_volts.start()
    load_table.start()

    barrier = pltpu.get_barrier_semaphore()
    z_peers = [grid_device(x_hi, y, lax.rem(z + d, 8), block) for d in range(1, 8)]
    y_peers = [grid_device(x_hi, lax.rem(y + d, 4), z, block) for d in range(1, 4)]
    x_peers = [
        grid_device(lax.rem(x_hi + d // 4, 2), y, z, lax.rem(block + d % 4, 4)) for d in range(1, 8)
    ]
    for peer in x_peers + y_peers + z_peers:
        pl.semaphore_signal(barrier, inc=1, device_id=peer, device_id_type=MESH)

    load_volts.wait()

    def filter_frames(first, read):
        for part in range(FRAME // LANES):
            lane = part * LANES
            rows = [read(d, lane).astype(jnp.float32) for d in range(-(TAPS - 1), TAPS)]
            taps = [taps_ref[p : p + 1, lane : lane + LANES] for p in range(TAPS)]
            for t in range(TAPS):
                total = taps[0] * rows[t]
                for p in range(1, TAPS):
                    total = total + taps[p] * rows[t + p]
                for half in range(2):
                    filt32[part, pl.ds(half * frames + first + t, 8, stride=2 * frames), :] = total[
                        half * 8 : half * 8 + 8
                    ]

    def read_volts(first):
        def read(d, lane):
            start = pl.multiple_of((first + d) * FRAME, FRAME) + lane
            return volts[:, pl.ds(start, LANES)]

        return read

    def filter_blocks(low, high):
        @pl.loop(low, high)
        def _(b):
            first = pl.multiple_of(b * TAPS, TAPS)
            filter_frames(first, read_volts(first))

    halo_copy = pltpu.make_async_remote_copy(
        src_ref=volts.at[:, pl.ds(frames * FRAME - HALO, HALO)],
        dst_ref=halo,
        send_sem=halo_send,
        recv_sem=halo_recv,
        device_id=(lax.axis_index("inputs"), lax.rem(block + 1, blocks)),
        device_id_type=MESH,
    )

    filter_blocks(1, 4)
    pl.semaphore_wait(barrier, len(x_peers + y_peers + z_peers))

    @pl.when(block < blocks - 1)
    def _():
        halo_copy.start()

    for peer in y_peers:
        pl.semaphore_signal(y_sem, inc=1, device_id=peer, device_id_type=MESH)
    filter_blocks(4, 6)
    pl.semaphore_wait(y_sem, len(y_peers))
    for peer in x_peers:
        pl.semaphore_signal(x_sem, inc=1, device_id=peer, device_id_type=MESH)
    filter_blocks(6, frames // TAPS)

    @pl.when(block > 0)
    def _():
        halo_copy.wait_recv()

    @pl.when(block == 0)
    def _():
        halo[...] = jnp.zeros_like(halo)

    def read_first(d, lane):
        if d < 0:
            return halo[:, (d + TAPS - 1) * FRAME + lane : (d + TAPS - 1) * FRAME + lane + LANES]
        return volts[:, d * FRAME + lane : d * FRAME + lane + LANES]

    filter_frames(0, read_first)
    for part in range(FRAME // LANES):
        filt[:, part * LANES : (part + 1) * LANES] = filt32[part].astype(jnp.bfloat16)
    load_table.wait()

    low = lax.broadcasted_iota(jnp.int32, (8, LANES), 1) < LANES // 2

    me = lax.axis_index("inputs")
    slot = pl.multiple_of((block * groups + me) * inp, inp)

    def transform(j):
        owner = lax.rem(block + j, blocks)
        rows = table[pl.ds(pl.multiple_of(owner * 2 * groups, 2 * groups), 2 * groups), :]
        for q in range(4):
            spec = lax.dot_general(
                rows,
                filt[q * 256 : (q + 1) * 256, :],
                (((1,), (1,)), ((), ())),
                preferred_element_type=jnp.float32,
            )
            for u in range(2):
                pair = 2 * q + u
                for g in range(groups // 8):
                    re = spec[g * 8 : g * 8 + 8, u * LANES : (u + 1) * LANES]
                    im = spec[groups + g * 8 : groups + g * 8 + 8, u * LANES : (u + 1) * LANES]
                    first = jnp.where(low, re, pltpu.roll(im, LANES // 2, 1))
                    second = jnp.where(low, pltpu.roll(re, LANES // 2, 1), im)
                    base = g * 8 * inp + pair
                    stage[pl.ds(base, 8, stride=inp), :] = first
                    stage[pl.ds(base + 8, 8, stride=inp), :] = second
        send[j] = stage[...].astype(jnp.bfloat16)

    def copy_to(j, device, row):
        return pltpu.make_async_remote_copy(
            src_ref=send.at[j, pl.ds(pl.multiple_of(row * inp, inp), inp)],
            dst_ref=recv.at[pl.ds(slot, inp)],
            send_sem=send_sem,
            recv_sem=recv_sem,
            device_id=device,
            device_id_type=MESH,
        )

    for j in range(blocks):
        transform(j)
        if j == 0:
            pl.semaphore_wait(x_sem, len(x_peers))

        @pl.loop(1 if j == 0 else 0, groups)
        def _(s):
            tx = lax.rem(x_hi + s // 32, 2)
            ty = lax.rem(y + (s // 8) % 4, 4)
            tz = lax.rem(z + s % 8, 8)
            row = tx * 32 + ty * 8 + tz
            copy_to(j, (row, lax.rem(block + j, blocks)), row).start()

        if j == 0:
            recv[pl.ds(slot, inp), :] = send[0, pl.ds(pl.multiple_of(me * inp, inp), inp), :]

    @pl.when(block < blocks - 1)
    def _():
        halo_copy.wait_send()

    count = (blocks * groups - 1) * inp
    drain = pltpu.make_async_remote_copy(
        src_ref=recv.at[pl.ds(0, count)],
        dst_ref=recv.at[pl.ds(0, count)],
        send_sem=send_sem,
        recv_sem=recv_sem,
        device_id=(me, lax.rem(block + 1, blocks)),
        device_id_type=MESH,
    )
    drain.wait_send()
    drain.wait_recv()


def channelize(voltages, pfb_taps, table):
    inp, samples = voltages.shape
    frames = samples // FRAME
    rows = inp * frames
    return pl.pallas_call(
        functools.partial(channel_kernel, frames),
        out_shape=jax.ShapeDtypeStruct((256 * inp, LANES), jnp.bfloat16),
        in_specs=[
            pl.BlockSpec(memory_space=pl.ANY),
            pl.BlockSpec(memory_space=pltpu.VMEM),
            pl.BlockSpec(memory_space=pl.ANY),
        ],
        out_specs=pl.BlockSpec(memory_space=pltpu.VMEM),
        scratch_shapes=[
            pltpu.VMEM((inp, samples), jnp.bfloat16),
            pltpu.VMEM((2 * F, FRAME), jnp.bfloat16),
            pltpu.VMEM((inp, HALO), jnp.bfloat16),
            pltpu.VMEM((FRAME // LANES, rows, LANES), jnp.float32),
            pltpu.VMEM((rows, FRAME), jnp.bfloat16),
            pltpu.VMEM((64 * inp, LANES), jnp.float32),
            pltpu.VMEM((4, 64 * inp, LANES), jnp.bfloat16),
            pltpu.SemaphoreType.DMA((2,)),
            pltpu.SemaphoreType.DMA,
            pltpu.SemaphoreType.DMA,
            pltpu.SemaphoreType.DMA,
            pltpu.SemaphoreType.DMA,
            pltpu.SemaphoreType.REGULAR,
            pltpu.SemaphoreType.REGULAR,
        ],
        compiler_params=pltpu.CompilerParams(
            collective_id=0, has_side_effects=True, vmem_limit_bytes=32 << 20
        ),
    )(voltages, pfb_taps, table)


def tile_kernel(scale, spec_ref, out_hbm, tiles, sem):
    blocks, count_in, lanes = spec_ref.shape
    nt = count_in // TILE
    left = jnp.concatenate([spec_ref[b] for b in range(blocks)], axis=-1)
    sign = jnp.where(lax.broadcasted_iota(jnp.int32, (1, lanes), 1) < lanes // 2, 1.0, -1.0)
    side = 2 * TILE
    copies = []
    pair = 0
    for big in range(nt // 2):
        rows = slice(big * side, (big + 1) * side)
        twisted = jnp.concatenate(
            [
                (pltpu.roll(spec_ref[b, rows].astype(jnp.float32), lanes // 2, 1) * sign).astype(
                    jnp.bfloat16
                )
                for b in range(blocks)
            ],
            axis=-1,
        )
        both = jnp.concatenate([left[rows], twisted], axis=0)
        first_pair = pair
        for cb in range(big, nt // 2):
            prod = lax.dot_general(
                both,
                left[cb * side : (cb + 1) * side],
                (((1,), (1,)), ((), ())),
                preferred_element_type=jnp.float32,
            ) * scale
            for a in range(2):
                for b in range(2):
                    row, col = 2 * big + a, 2 * cb + b
                    if col < row:
                        continue
                    place = row * nt - row * (row - 1) // 2 + col - row
                    for c in range(2):
                        lo = c * side + a * TILE
                        tiles[place, c] = prod[lo : lo + TILE, b * TILE : (b + 1) * TILE]
        pair = (2 * big + 2) * nt - (2 * big + 2) * (2 * big + 1) // 2
        copy = pltpu.make_async_copy(
            tiles.at[first_pair:pair], out_hbm.at[0, first_pair:pair], sem.at[big]
        )
        copy.start()
        copies.append(copy)
    for copy in copies:
        copy.wait()


def tile_sums(spec, scale):
    nt = spec.shape[1] // TILE
    pairs = nt * (nt + 1) // 2
    return pl.pallas_call(
        functools.partial(tile_kernel, scale),
        out_shape=jax.ShapeDtypeStruct((1, pairs, 2, TILE, TILE), jnp.float32),
        in_specs=[pl.BlockSpec(memory_space=pltpu.VMEM)],
        out_specs=pl.BlockSpec(memory_space=pl.ANY),
        scratch_shapes=[
            pltpu.VMEM((pairs, 2, TILE, TILE), jnp.float32),
            pltpu.SemaphoreType.DMA((nt // 2,)),
        ],
        compiler_params=pltpu.CompilerParams(vmem_limit_bytes=32 << 20),
    )(spec)


def on_device(voltages, pfb_taps):
    table = jnp.asarray(dft_table(F, FRAME, lax.axis_size("tm")))
    frames = voltages.shape[1] // FRAME
    turned = channelize(voltages, pfb_taps, table)
    spec = turned.reshape(lax.axis_size("tm"), lax.axis_size("inputs") * voltages.shape[0], LANES)
    return tile_sums(spec, 1.0 / (frames * lax.axis_size("tm")))


def solution(mesh):
    in_specs = (P("inputs", "tm"), P())
    out_specs = P(("inputs", "tm"), None, None, None, None)
    return jax.shard_map(
        on_device, mesh=mesh, in_specs=in_specs, out_specs=out_specs, check_vma=False
    )
```

time: 324 us -> 46.7 us (0.14)
  waiting for transfers between devices: 162 us -> 0 us
  local copies, waits for them, and re-layouts: 56.1 us -> 2.98 us
  Pallas kernels: 0 us -> 43.5 us
  blocking collectives: 42.6 us -> 0 us
  matrix products: 29.9 us -> 0 us
  other arithmetic: 14.7 us -> 0 us
  between operations: 13.5 us -> 0.01 us
  starting transfers between devices: 4.5 us -> 0 us
    reduce_scatter x1 -> x0, waiting for transfers between devices: 161 us -> none  [on_device(): lax.psum_scatter(tile_sums(turned, scale), 'tm', scatter_dimension=0, til...]
    pallas_call x0 -> x2, Pallas kernels: none -> 43.5 us  [the longest x1 40.5 us: channelize(): pl.pallas_call(functools.partial(channel_kernel, frames), out_shape=jax.S...]
    all_to_all x1 -> x0, blocking collectives: 42.6 us -> none  [on_device(): lax.all_to_all(spectra, 'inputs', split_axis=0, concat_axis=2, tiled=True)]
    dot_general x17 -> x0, matrix products: 29.9 us -> none  [the longest x8 12.4 us: tile_sums(): jnp.einsum('cik,cjk->cij', twisted[:, lower:lower + TILE], cols, preferre...]
    unnamed x36 -> x6, local copies, waits for them, and re-layouts: 29.1 us -> 2.98 us
    transpose x8 -> x0, local copies, waits for them, and re-layouts: 21.8 us -> none  [the longest x4 10.9 us: tile_sums(): real_part.reshape(chans, TILE, count, TILE).transpose(0, 2, 1, 3)]
    mul x1 -> x0, other arithmetic: 13.3 us -> none  [tile_sums(): return jnp.stack([real_all, imag_all], axis=2) * scale]
    ppermute x1 -> x0, starting transfers between devices: 4.5 us -> none  [from_behind(): lax.ppermute(value, axis, [(source, source + steps) for source in range(i...]
  transfers between devices with their start and end apart: 2 -> 0, of which waited for: 2 -> 0; matrix products, arithmetic and copies ran while one was open for 0% -> 0% of each run, Pallas kernels for 0% -> 0%
where the time goes in v1:
time: 46.7 us; the launch traced here: 46.5 us
  Pallas kernels  43.5 us (93%)
  local copies, waits for them, and re-layouts  2.98 us (6%)
    pallas_call x1, Pallas kernels, channelize(): pl.pallas_call(functools.partial(channel_kernel, frames), out_shape=jax.S...  40.5 us
    unnamed x6, local copies, waits for them, and re-layouts  2.98 us
    pallas_call x1, Pallas kernels, tile_sums(): pl.pallas_call(functools.partial(tile_kernel, scale), out_shape=jax.Shape...  2.95 us

profile of v1, /device:TPU:1, one launch (start us, length us, event | category | flops | bytes accessed | tf_op | source)
XLA Modules:
  0.0 46.5 jit_solution(4435236638779657057)
XLA Ops:
  0.0 0.0 copy-start
  0.0 1.2 %copy-done = bf16[16,32768]{1,0:T(8,128)(2,1)S(1)} copy-done((bf16[16,32768]{1,0:T(8,128)(2,1)S(1)}, bf16[16,32768]{1,0:T(8,128)(2,1)}, u32[]{:S(2)}) %copy-start) | copy-done | bytes 1048600
  1.2 0.0 copy-start.1
  1.2 1.0 %copy-done.1 = bf16[512,512]{1,0:T(8,128)(2,1)S(1)} copy-done((bf16[512,512]{1,0:T(8,128)(2,1)S(1)}, bf16[512,512]{1,0:T(8,128)(2,1)}, u32[]{:S(2)}) %copy-start.1) | copy-done | bytes 524312
  2.3 0.0 copy-start.2
  2.3 0.7 %copy-done.2 = f32[8,512]{1,0:T(8,128)S(1)} copy-done((f32[8,512]{1,0:T(8,128)S(1)}, f32[8,512]{1,0:T(8,128)}, u32[]{:S(2)}) %copy-start.2) | copy-done | bytes 16408
  3.0 40.5 %shard_map.37 = bf16[4096,128]{1,0:T(8,128)(2,1)S(1)} custom-call(bf16[16,32768]{1,0:T(8,128)(2,1)S(1)} %copy-done, f32[8,512]{1,0:T(8,128)S(1)} %copy-done.2, bf16[512,512]{1,0:T(8,128)(2,1)S(1)} %copy-done.1), custom_call_target="tpu_custom_call" | custom-call | tf_op jit(solution)/shard_map/pallas_call | solution.py:209
  43.5 3.0 %shard_map.38 = f32[1,36,2,128,128]{4,3,2,1,0:T(8,128)} custom-call(bf16[4,1024,128]{2,1,0:T(8,128)(2,1)S(1)} %bitcast.1), custom_call_target="tpu_custom_call" | custom-call | tf_op jit(solution)/shard_map/pallas_call | solution.py:290
Async XLA Ops:
  0.0 1.2 %copy-start = (bf16[16,32768]{1,0:T(8,128)(2,1)S(1)}, bf16[16,32768]{1,0:T(8,128)(2,1)}, u32[]{:S(2)}) copy-start(bf16[16,32768]{1,0:T(8,128)(2,1)} %v_hbm.1) | copy-start | bytes 3145732
  1.2 1.0 %copy-start.1 = (bf16[512,512]{1,0:T(8,128)(2,1)S(1)}, bf16[512,512]{1,0:T(8,128)(2,1)}, u32[]{:S(2)}) copy-start(bf16[512,512]{1,0:T(8,128)(2,1)} %constant.2.clone.table_hbm) | copy-start | bytes 1572868
  2.3 0.7 %copy-start.2 = (f32[8,512]{1,0:T(8,128)S(1)}, f32[8,512]{1,0:T(8,128)}, u32[]{:S(2)}) copy-start(f32[8,512]{1,0:T(8,128)} %taps_ref.1) | copy-start | bytes 49156

commit v2 on v1

--- a/solution.py
+++ b/solution.py
@@ -14,6 +14,9 @@
 FRAME = 512
 HALO = (TAPS - 1) * FRAME
 LANES = 128
+CHUNKS = 4
+TABLE_COPIES = 3
+VMEM_BYTES = 55312384
 MESH = pl.DeviceIdType.MESH
 
 
@@ -24,7 +27,8 @@
     angle = 2.0 * np.pi / length * phase.astype(np.float64)
     vals = np.stack([np.cos(angle), -np.sin(angle)]) / length**0.5
     vals = vals.reshape(2, chans // owners, owners, length).transpose(2, 0, 1, 3)
-    return vals.reshape(2 * chans, length).astype(np.float32).astype(jnp.bfloat16)
+    vals = vals.reshape(2 * chans, length).astype(np.float32).astype(jnp.bfloat16)
+    return np.concatenate([vals] * TABLE_COPIES)
 
 
 def grid_coords():
@@ -38,8 +42,8 @@
 
 
 def channel_kernel(
-    frames, v_hbm, taps_ref, table_hbm, recv,
-    volts, table, halo, filt32, filt, stage, send,
+    frames, v_hbm, taps_hbm, table_hbm, recv,
+    volts, taps_ref, table, halo, filt32, filt, stage, send,
     in_sems, halo_send, halo_recv, send_sem, recv_sem, y_sem, x_sem,
 ):
     x_hi, y, z, block = grid_coords()
@@ -47,10 +51,16 @@
     groups = 64
     inp = v_hbm.shape[0]
 
-    load_volts = pltpu.make_async_copy(v_hbm, volts, in_sems.at[0])
-    load_table = pltpu.make_async_copy(table_hbm, table, in_sems.at[1])
-    load_volts.start()
-    load_table.start()
+    chunk = frames // CHUNKS
+    load_volts = []
+    for c in range(CHUNKS):
+        part = pl.ds(c * chunk * FRAME, chunk * FRAME)
+        load_volts.append(pltpu.make_async_copy(v_hbm.at[:, part], volts.at[:, part], in_sems.at[c]))
+    load_taps = pltpu.make_async_copy(taps_hbm, taps_ref, in_sems.at[CHUNKS])
+    load_table = pltpu.make_async_copy(table_hbm.at[0 : 2 * F], table, in_sems.at[CHUNKS + 1])
+    load_taps.start()
+    for load in load_volts:
+        load.start()
 
     barrier = pltpu.get_barrier_semaphore()
     z_peers = [grid_device(x_hi, y, lax.rem(z + d, 8), block) for d in range(1, 8)]
@@ -58,10 +68,11 @@
     x_peers = [
         grid_device(lax.rem(x_hi + d // 4, 2), y, z, lax.rem(block + d % 4, 4)) for d in range(1, 8)
     ]
-    for peer in x_peers + y_peers + z_peers:
+    for peer in z_peers + y_peers + x_peers:
         pl.semaphore_signal(barrier, inc=1, device_id=peer, device_id_type=MESH)
 
-    load_volts.wait()
+    load_table.start()
+    load_taps.wait()
 
     def filter_frames(first, read):
         for part in range(FRAME // LANES):
@@ -91,7 +102,7 @@
             filter_frames(first, read_volts(first))
 
     halo_copy = pltpu.make_async_remote_copy(
-        src_ref=volts.at[:, pl.ds(frames * FRAME - HALO, HALO)],
+        src_ref=v_hbm.at[:, pl.ds(frames * FRAME - HALO, HALO)],
         dst_ref=halo,
         send_sem=halo_send,
         recv_sem=halo_recv,
@@ -99,7 +110,7 @@
         device_id_type=MESH,
     )
 
-    filter_blocks(1, 4)
+    load_volts[0].wait()
     pl.semaphore_wait(barrier, len(x_peers + y_peers + z_peers))
 
     @pl.when(block < blocks - 1)
@@ -108,11 +119,14 @@
 
     for peer in y_peers:
         pl.semaphore_signal(y_sem, inc=1, device_id=peer, device_id_type=MESH)
-    filter_blocks(4, 6)
+    per = chunk // TAPS
+    filter_blocks(1, per)
+    for c in range(1, CHUNKS):
+        load_volts[c].wait()
+        filter_blocks(c * per, (c + 1) * per)
     pl.semaphore_wait(y_sem, len(y_peers))
     for peer in x_peers:
         pl.semaphore_signal(x_sem, inc=1, device_id=peer, device_id_type=MESH)
-    filter_blocks(6, frames // TAPS)
 
     @pl.when(block > 0)
     def _():
@@ -128,8 +142,6 @@
         return volts[:, d * FRAME + lane : d * FRAME + lane + LANES]
 
     filter_frames(0, read_first)
-    for part in range(FRAME // LANES):
-        filt[:, part * LANES : (part + 1) * LANES] = filt32[part].astype(jnp.bfloat16)
     load_table.wait()
 
     low = lax.broadcasted_iota(jnp.int32, (8, LANES), 1) < LANES // 2
@@ -141,9 +153,14 @@
         owner = lax.rem(block + j, blocks)
         rows = table[pl.ds(pl.multiple_of(owner * 2 * groups, 2 * groups), 2 * groups), :]
         for q in range(4):
+            quarter = slice(q * 256, (q + 1) * 256)
+            if j == 0:
+                filt[quarter, :] = jnp.concatenate(
+                    [filt32[part, quarter, :] for part in range(FRAME // LANES)], axis=1
+                ).astype(jnp.bfloat16)
             spec = lax.dot_general(
                 rows,
-                filt[q * 256 : (q + 1) * 256, :],
+                filt[quarter, :],
                 (((1,), (1,)), ((), ())),
                 preferred_element_type=jnp.float32,
             )
@@ -169,21 +186,24 @@
             device_id_type=MESH,
         )
 
+    def send_range(j, low_step, high_step, turn):
+        @pl.loop(low_step, high_step)
+        def _(s):
+            tx = lax.rem(x_hi + s // 32 + turn * (s // 4), 2)
+            ty = lax.rem(y + s // 8 + s, 4)
+            tz = lax.rem(z + s, 8)
+            row = tx * 32 + ty * 8 + tz
+            copy_to(j, (row, lax.rem(block + j, blocks)), row).start()
+
     for j in range(blocks):
         transform(j)
         if j == 0:
+            send_range(j, 1, groups // 2, 0)
             pl.semaphore_wait(x_sem, len(x_peers))
-
-        @pl.loop(1 if j == 0 else 0, groups)
-        def _(s):
-            tx = lax.rem(x_hi + s // 32, 2)
-            ty = lax.rem(y + (s // 8) % 4, 4)
-            tz = lax.rem(z + s % 8, 8)
-            row = tx * 32 + ty * 8 + tz
-            copy_to(j, (row, lax.rem(block + j, blocks)), row).start()
-
-        if j == 0:
+            send_range(j, groups // 2, groups, 0)
             recv[pl.ds(slot, inp), :] = send[0, pl.ds(pl.multiple_of(me * inp, inp), inp), :]
+        else:
+            send_range(j, 0, groups, 1)
 
     @pl.when(block < blocks - 1)
     def _():
@@ -210,20 +230,21 @@
         functools.partial(channel_kernel, frames),
         out_shape=jax.ShapeDtypeStruct((256 * inp, LANES), jnp.bfloat16),
         in_specs=[
-            pl.BlockSpec(memory_space=pl.ANY),
-            pl.BlockSpec(memory_space=pltpu.VMEM),
-            pl.BlockSpec(memory_space=pl.ANY),
+            pl.BlockSpec(memory_space=pltpu.HBM),
+            pl.BlockSpec(memory_space=pltpu.HBM),
+            pl.BlockSpec(memory_space=pltpu.HBM),
         ],
         out_specs=pl.BlockSpec(memory_space=pltpu.VMEM),
         scratch_shapes=[
             pltpu.VMEM((inp, samples), jnp.bfloat16),
+            pltpu.VMEM((TAPS, FRAME), jnp.float32),
             pltpu.VMEM((2 * F, FRAME), jnp.bfloat16),
             pltpu.VMEM((inp, HALO), jnp.bfloat16),
             pltpu.VMEM((FRAME // LANES, rows, LANES), jnp.float32),
             pltpu.VMEM((rows, FRAME), jnp.bfloat16),
             pltpu.VMEM((64 * inp, LANES), jnp.float32),
             pltpu.VMEM((4, 64 * inp, LANES), jnp.bfloat16),
-            pltpu.SemaphoreType.DMA((2,)),
+            pltpu.SemaphoreType.DMA((CHUNKS + 2,)),
             pltpu.SemaphoreType.DMA,
             pltpu.SemaphoreType.DMA,
             pltpu.SemaphoreType.DMA,
@@ -232,7 +253,7 @@
             pltpu.SemaphoreType.REGULAR,
         ],
         compiler_params=pltpu.CompilerParams(
-            collective_id=0, has_side_effects=True, vmem_limit_bytes=32 << 20
+            collective_id=0, has_side_effects=True, vmem_limit_bytes=VMEM_BYTES
         ),
     )(voltages, pfb_taps, table)
 
@@ -244,7 +265,6 @@
     sign = jnp.where(lax.broadcasted_iota(jnp.int32, (1, lanes), 1) < lanes // 2, 1.0, -1.0)
     side = 2 * TILE
     copies = []
-    pair = 0
     for big in range(nt // 2):
         rows = slice(big * side, (big + 1) * side)
         twisted = jnp.concatenate(
@@ -257,7 +277,6 @@
             axis=-1,
         )
         both = jnp.concatenate([left[rows], twisted], axis=0)
-        first_pair = pair
         for cb in range(big, nt // 2):
             prod = lax.dot_general(
                 both,
@@ -274,12 +293,14 @@
                     for c in range(2):
                         lo = c * side + a * TILE
                         tiles[place, c] = prod[lo : lo + TILE, b * TILE : (b + 1) * TILE]
-        pair = (2 * big + 2) * nt - (2 * big + 2) * (2 * big + 1) // 2
-        copy = pltpu.make_async_copy(
-            tiles.at[first_pair:pair], out_hbm.at[0, first_pair:pair], sem.at[big]
-        )
-        copy.start()
-        copies.append(copy)
+                first = max(row, 2 * cb)
+                place = row * nt - row * (row - 1) // 2 + first - row
+                pairs = slice(place, place + 2 * cb + 2 - first)
+                copy = pltpu.make_async_copy(
+                    tiles.at[pairs], out_hbm.at[0, pairs], sem.at[len(copies)]
+                )
+                copy.start()
+                copies.append(copy)
     for copy in copies:
         copy.wait()
 
@@ -294,7 +315,7 @@
         out_specs=pl.BlockSpec(memory_space=pl.ANY),
         scratch_shapes=[
             pltpu.VMEM((pairs, 2, TILE, TILE), jnp.float32),
-            pltpu.SemaphoreType.DMA((nt // 2,)),
+            pltpu.SemaphoreType.DMA((nt // 2 * (nt // 2 + 1),)),
         ],
         compiler_params=pltpu.CompilerParams(vmem_limit_bytes=32 << 20),
     )(spec)

time: 46.7 us -> 43.4 us (0.929)
  local copies, waits for them, and re-layouts: 2.98 us -> 0.72 us
  Pallas kernels: 43.5 us -> 42.5 us
    unnamed x6 -> x2, local copies, waits for them, and re-layouts: 2.98 us -> 0.72 us
    pallas_call x1, Pallas kernels: 40.5 us -> 39.7 us  [channelize(): pl.pallas_call(functools.partial(channel_kernel, frames), out_shape=jax.S...]
where the time goes in v2:
time: 43.4 us; the launch traced here: 43.3 us
  Pallas kernels  42.5 us (98%)
  local copies, waits for them, and re-layouts  0.72 us (2%)
    pallas_call x1, Pallas kernels, channelize(): pl.pallas_call(functools.partial(channel_kernel, frames), out_shape=jax.S...  39.7 us
    pallas_call x1, Pallas kernels, tile_sums(): pl.pallas_call(functools.partial(tile_kernel, scale), out_shape=jax.Shape...  2.79 us

profile of v2, /device:TPU:1, one launch (start us, length us, event | category | flops | bytes accessed | tf_op | source)
XLA Modules:
  0.0 43.3 jit_solution(1638526680572491455)
XLA Ops:
  0.0 0.0 copy-start
  0.0 0.7 %copy-done = f32[8,512]{1,0:T(8,128)S(1)} copy-done((f32[8,512]{1,0:T(8,128)S(1)}, f32[8,512]{1,0:T(8,128)}, u32[]{:S(2)}) %copy-start) | copy-done | bytes 16408
  0.7 39.7 %shard_map.37 = bf16[4096,128]{1,0:T(8,128)(2,1)S(1)} custom-call(bf16[16,32768]{1,0:T(8,128)(2,1)} %v_hbm.1, f32[8,512]{1,0:T(8,128)S(1)} %copy-done, bf16[1536,512]{1,0:T(8,128)(2,1)} %constant.2.clone.table_hbm), custom_call_target="tpu_custom_call" | custom-call | tf_op jit(solution)/shard_map/pallas_call | solution.py:229
  40.5 2.8 %shard_map.38 = f32[1,36,2,128,128]{4,3,2,1,0:T(8,128)} custom-call(bf16[4,1024,128]{2,1,0:T(8,128)(2,1)S(1)} %bitcast.1), custom_call_target="tpu_custom_call" | custom-call | tf_op jit(solution)/shard_map/pallas_call | solution.py:311
Async XLA Ops:
  0.0 0.7 %copy-start = (f32[8,512]{1,0:T(8,128)S(1)}, f32[8,512]{1,0:T(8,128)}, u32[]{:S(2)}) copy-start(f32[8,512]{1,0:T(8,128)} %taps_hbm.1) | copy-start | bytes 49156

commit v3 on v2

--- a/solution.py
+++ b/solution.py
@@ -14,9 +14,12 @@
 FRAME = 512
 HALO = (TAPS - 1) * FRAME
 LANES = 128
-CHUNKS = 4
+CHUNKS = 8
+EARLY = 3
+PITCH = 136
+PARTS = 6
 TABLE_COPIES = 3
-VMEM_BYTES = 55312384
+VMEM_BYTES = 51298304
 MESH = pl.DeviceIdType.MESH
 
 
@@ -42,10 +45,13 @@
 
 
 def channel_kernel(
-    frames, v_hbm, taps_hbm, table_hbm, recv,
-    volts, taps_ref, table, halo, filt32, filt, stage, send,
-    in_sems, halo_send, halo_recv, send_sem, recv_sem, y_sem, x_sem,
+    frames, v_hbm, taps_hbm, table_hbm, late, *refs
 ):
+    sums = refs[:PARTS]
+    (
+        volts, taps_ref, table, halo, filt32, filt, stage, send, early,
+        in_sems, halo_send, halo_recv, send_sem, recv_sems, y_sem, x_sem,
+    ) = refs[PARTS:]
     x_hi, y, z, block = grid_coords()
     blocks = 4
     groups = 64
@@ -68,11 +74,10 @@
     x_peers = [
         grid_device(lax.rem(x_hi + d // 4, 2), y, z, lax.rem(block + d % 4, 4)) for d in range(1, 8)
     ]
-    for peer in z_peers + y_peers + x_peers:
+    for peer in x_peers + z_peers + y_peers:
         pl.semaphore_signal(barrier, inc=1, device_id=peer, device_id_type=MESH)
 
     load_table.start()
-    load_taps.wait()
 
     def filter_frames(first, read):
         for part in range(FRAME // LANES):
@@ -84,7 +89,7 @@
                 for p in range(1, TAPS):
                     total = total + taps[p] * rows[t + p]
                 for half in range(2):
-                    filt32[part, pl.ds(half * frames + first + t, 8, stride=2 * frames), :] = total[
+                    filt32[part, pl.ds(half * frames + first + t, 8, stride=PITCH), :] = total[
                         half * 8 : half * 8 + 8
                     ]
 
@@ -110,7 +115,6 @@
         device_id_type=MESH,
     )
 
-    load_volts[0].wait()
     pl.semaphore_wait(barrier, len(x_peers + y_peers + z_peers))
 
     @pl.when(block < blocks - 1)
@@ -120,6 +124,8 @@
     for peer in y_peers:
         pl.semaphore_signal(y_sem, inc=1, device_id=peer, device_id_type=MESH)
     per = chunk // TAPS
+    load_taps.wait()
+    load_volts[0].wait()
     filter_blocks(1, per)
     for c in range(1, CHUNKS):
         load_volts[c].wait()
@@ -147,7 +153,8 @@
     low = lax.broadcasted_iota(jnp.int32, (8, LANES), 1) < LANES // 2
 
     me = lax.axis_index("inputs")
-    slot = pl.multiple_of((block * groups + me) * inp, inp)
+    span = groups * inp
+    slot = pl.multiple_of(me * inp, inp)
 
     def transform(j):
         owner = lax.rem(block + j, blocks)
@@ -156,7 +163,17 @@
             quarter = slice(q * 256, (q + 1) * 256)
             if j == 0:
                 filt[quarter, :] = jnp.concatenate(
-                    [filt32[part, quarter, :] for part in range(FRAME // LANES)], axis=1
+                    [
+                        jnp.concatenate(
+                            [
+                                filt32[part, pair * PITCH : pair * PITCH + 2 * frames, :]
+                                for pair in (2 * q, 2 * q + 1)
+                            ],
+                            axis=0,
+                        )
+                        for part in range(FRAME // LANES)
+                    ],
+                    axis=1,
                 ).astype(jnp.bfloat16)
             spec = lax.dot_general(
                 rows,
@@ -174,14 +191,16 @@
                     base = g * 8 * inp + pair
                     stage[pl.ds(base, 8, stride=inp), :] = first
                     stage[pl.ds(base + 8, 8, stride=inp), :] = second
-        send[j] = stage[...].astype(jnp.bfloat16)
+        send[j * span : (j + 1) * span, :] = stage[...].astype(jnp.bfloat16)
 
     def copy_to(j, device, row):
         return pltpu.make_async_remote_copy(
-            src_ref=send.at[j, pl.ds(pl.multiple_of(row * inp, inp), inp)],
-            dst_ref=recv.at[pl.ds(slot, inp)],
+            src_ref=send.at[pl.ds(pl.multiple_of(j * span + row * inp, inp), inp)],
+            dst_ref=early.at[pl.ds(j * span + slot, inp)]
+            if j < EARLY
+            else late.at[j - EARLY, pl.ds(slot, inp)],
             send_sem=send_sem,
-            recv_sem=recv_sem,
+            recv_sem=recv_sems.at[0 if j < EARLY else 1],
             device_id=device,
             device_id_type=MESH,
         )
@@ -201,7 +220,7 @@
             send_range(j, 1, groups // 2, 0)
             pl.semaphore_wait(x_sem, len(x_peers))
             send_range(j, groups // 2, groups, 0)
-            recv[pl.ds(slot, inp), :] = send[0, pl.ds(pl.multiple_of(me * inp, inp), inp), :]
+            early[pl.ds(slot, inp), :] = send[pl.ds(slot, inp), :]
         else:
             send_range(j, 0, groups, 1)
 
@@ -209,70 +228,43 @@
     def _():
         halo_copy.wait_send()
 
-    count = (blocks * groups - 1) * inp
-    drain = pltpu.make_async_remote_copy(
-        src_ref=recv.at[pl.ds(0, count)],
-        dst_ref=recv.at[pl.ds(0, count)],
-        send_sem=send_sem,
-        recv_sem=recv_sem,
-        device_id=(me, lax.rem(block + 1, blocks)),
-        device_id_type=MESH,
+    def arrivals(ref, sem):
+        return pltpu.make_async_remote_copy(
+            src_ref=ref,
+            dst_ref=ref,
+            send_sem=send_sem,
+            recv_sem=recv_sems.at[sem],
+            device_id=(me, lax.rem(block + 1, blocks)),
+            device_id_type=MESH,
+        )
+
+    arrivals(early.at[0 : EARLY * span - inp], 0).wait_recv()
+
+    def keep(place, c, prod):
+        sums[place // (36 // PARTS)][place % (36 // PARTS), c] = prod
+
+    tile_products(
+        [early.at[j * span : (j + 1) * span] for j in range(EARLY)], keep, lambda *_: None
     )
-    drain.wait_send()
-    drain.wait_recv()
-
-
-def channelize(voltages, pfb_taps, table):
-    inp, samples = voltages.shape
-    frames = samples // FRAME
-    rows = inp * frames
-    return pl.pallas_call(
-        functools.partial(channel_kernel, frames),
-        out_shape=jax.ShapeDtypeStruct((256 * inp, LANES), jnp.bfloat16),
-        in_specs=[
-            pl.BlockSpec(memory_space=pltpu.HBM),
-            pl.BlockSpec(memory_space=pltpu.HBM),
-            pl.BlockSpec(memory_space=pltpu.HBM),
-        ],
-        out_specs=pl.BlockSpec(memory_space=pltpu.VMEM),
-        scratch_shapes=[
-            pltpu.VMEM((inp, samples), jnp.bfloat16),
-            pltpu.VMEM((TAPS, FRAME), jnp.float32),
-            pltpu.VMEM((2 * F, FRAME), jnp.bfloat16),
-            pltpu.VMEM((inp, HALO), jnp.bfloat16),
-            pltpu.VMEM((FRAME // LANES, rows, LANES), jnp.float32),
-            pltpu.VMEM((rows, FRAME), jnp.bfloat16),
-            pltpu.VMEM((64 * inp, LANES), jnp.float32),
-            pltpu.VMEM((4, 64 * inp, LANES), jnp.bfloat16),
-            pltpu.SemaphoreType.DMA((CHUNKS + 2,)),
-            pltpu.SemaphoreType.DMA,
-            pltpu.SemaphoreType.DMA,
-            pltpu.SemaphoreType.DMA,
-            pltpu.SemaphoreType.DMA,
-            pltpu.SemaphoreType.REGULAR,
-            pltpu.SemaphoreType.REGULAR,
-        ],
-        compiler_params=pltpu.CompilerParams(
-            collective_id=0, has_side_effects=True, vmem_limit_bytes=VMEM_BYTES
-        ),
-    )(voltages, pfb_taps, table)
-
-
-def tile_kernel(scale, spec_ref, out_hbm, tiles, sem):
-    blocks, count_in, lanes = spec_ref.shape
+
+    arrivals(send.at[0 : blocks * span - inp], 1).wait_send()
+    arrivals(late, 1).wait_recv()
+
+
+def tile_products(specs, keep, done):
+    count_in, lanes = specs[0].shape
     nt = count_in // TILE
-    left = jnp.concatenate([spec_ref[b] for b in range(blocks)], axis=-1)
+    left = jnp.concatenate([spec[...] for spec in specs], axis=-1)
     sign = jnp.where(lax.broadcasted_iota(jnp.int32, (1, lanes), 1) < lanes // 2, 1.0, -1.0)
     side = 2 * TILE
-    copies = []
     for big in range(nt // 2):
         rows = slice(big * side, (big + 1) * side)
         twisted = jnp.concatenate(
             [
-                (pltpu.roll(spec_ref[b, rows].astype(jnp.float32), lanes // 2, 1) * sign).astype(
+                (pltpu.roll(spec[rows, :].astype(jnp.float32), lanes // 2, 1) * sign).astype(
                     jnp.bfloat16
                 )
-                for b in range(blocks)
+                for spec in specs
             ],
             axis=-1,
         )
@@ -283,50 +275,103 @@
                 left[cb * side : (cb + 1) * side],
                 (((1,), (1,)), ((), ())),
                 preferred_element_type=jnp.float32,
-            ) * scale
+            )
             for a in range(2):
-                for b in range(2):
-                    row, col = 2 * big + a, 2 * cb + b
-                    if col < row:
-                        continue
-                    place = row * nt - row * (row - 1) // 2 + col - row
+                row = 2 * big + a
+                first = max(row, 2 * cb)
+                place = row * nt - row * (row - 1) // 2 + first - row
+                for col in range(first, 2 * cb + 2):
+                    b = col - 2 * cb
                     for c in range(2):
                         lo = c * side + a * TILE
-                        tiles[place, c] = prod[lo : lo + TILE, b * TILE : (b + 1) * TILE]
-                first = max(row, 2 * cb)
-                place = row * nt - row * (row - 1) // 2 + first - row
-                pairs = slice(place, place + 2 * cb + 2 - first)
-                copy = pltpu.make_async_copy(
-                    tiles.at[pairs], out_hbm.at[0, pairs], sem.at[len(copies)]
-                )
-                copy.start()
-                copies.append(copy)
+                        keep(
+                            place + col - first,
+                            c,
+                            prod[lo : lo + TILE, b * TILE : (b + 1) * TILE],
+                        )
+                done(place, place + 2 * cb + 2 - first)
+
+
+def channelize(voltages, pfb_taps, table):
+    inp, samples = voltages.shape
+    frames = samples // FRAME
+    rows = inp * frames
+    return pl.pallas_call(
+        functools.partial(channel_kernel, frames),
+        out_shape=[jax.ShapeDtypeStruct((4 - EARLY, 64 * inp, LANES), jnp.bfloat16)]
+        + [jax.ShapeDtypeStruct((36 // PARTS, 2, TILE, TILE), jnp.float32)] * PARTS,
+        in_specs=[
+            pl.BlockSpec(memory_space=pltpu.HBM),
+            pl.BlockSpec(memory_space=pltpu.HBM),
+            pl.BlockSpec(memory_space=pltpu.HBM),
+        ],
+        out_specs=[pl.BlockSpec(memory_space=pltpu.VMEM)] * (1 + PARTS),
+        scratch_shapes=[
+            pltpu.VMEM((inp, samples), jnp.bfloat16),
+            pltpu.VMEM((TAPS, FRAME), jnp.float32),
+            pltpu.VMEM((2 * F, FRAME), jnp.bfloat16),
+            pltpu.VMEM((inp, HALO), jnp.bfloat16),
+            pltpu.VMEM((FRAME // LANES, 8 * PITCH, LANES), jnp.float32),
+            pltpu.VMEM((rows, FRAME), jnp.bfloat16),
+            pltpu.VMEM((64 * inp, LANES), jnp.float32),
+            pltpu.VMEM((4 * 64 * inp, LANES), jnp.bfloat16),
+            pltpu.VMEM((EARLY * 64 * inp, LANES), jnp.bfloat16),
+            pltpu.SemaphoreType.DMA((CHUNKS + 2,)),
+            pltpu.SemaphoreType.DMA,
+            pltpu.SemaphoreType.DMA,
+            pltpu.SemaphoreType.DMA,
+            pltpu.SemaphoreType.DMA((2,)),
+            pltpu.SemaphoreType.REGULAR,
+            pltpu.SemaphoreType.REGULAR,
+        ],
+        compiler_params=pltpu.CompilerParams(
+            collective_id=0, has_side_effects=True, vmem_limit_bytes=VMEM_BYTES
+        ),
+    )(voltages, pfb_taps, table)
+
+
+def tile_kernel(scale, late, *refs):
+    sums = refs[:PARTS]
+    out_hbm, tiles, sem = refs[PARTS:]
+    copies = []
+
+    def keep(place, c, prod):
+        earlier = sums[place // (36 // PARTS)][place % (36 // PARTS), c]
+        tiles[place, c] = (earlier + prod) * scale
+
+    def done(low, high):
+        copy = pltpu.make_async_copy(
+            tiles.at[low:high], out_hbm.at[0, low:high], sem.at[len(copies)]
+        )
+        copy.start()
+        copies.append(copy)
+
+    tile_products([late.at[j] for j in range(late.shape[0])], keep, done)
     for copy in copies:
         copy.wait()
 
 
-def tile_sums(spec, scale):
-    nt = spec.shape[1] // TILE
+def tile_sums(late, sums, scale):
+    nt = late.shape[1] // TILE
     pairs = nt * (nt + 1) // 2
     return pl.pallas_call(
         functools.partial(tile_kernel, scale),
         out_shape=jax.ShapeDtypeStruct((1, pairs, 2, TILE, TILE), jnp.float32),
-        in_specs=[pl.BlockSpec(memory_space=pltpu.VMEM)],
+        in_specs=[pl.BlockSpec(memory_space=pltpu.VMEM)] * (1 + PARTS),
         out_specs=pl.BlockSpec(memory_space=pl.ANY),
         scratch_shapes=[
             pltpu.VMEM((pairs, 2, TILE, TILE), jnp.float32),
             pltpu.SemaphoreType.DMA((nt // 2 * (nt // 2 + 1),)),
         ],
         compiler_params=pltpu.CompilerParams(vmem_limit_bytes=32 << 20),
-    )(spec)
+    )(late, *sums)
 
 
 def on_device(voltages, pfb_taps):
     table = jnp.asarray(dft_table(F, FRAME, lax.axis_size("tm")))
     frames = voltages.shape[1] // FRAME
-    turned = channelize(voltages, pfb_taps, table)
-    spec = turned.reshape(lax.axis_size("tm"), lax.axis_size("inputs") * voltages.shape[0], LANES)
-    return tile_sums(spec, 1.0 / (frames * lax.axis_size("tm")))
+    late, *sums = channelize(voltages, pfb_taps, table)
+    return tile_sums(late, sums, 1.0 / (frames * lax.axis_size("tm")))
 
 
 def solution(mesh):

time: 43.4 us -> 42.8 us (0.986)
  Pallas kernels: 42.5 us -> 41.9 us
where the time goes in v3:
time: 42.8 us; the launch traced here: 42.6 us
  Pallas kernels  41.9 us (98%)
  local copies, waits for them, and re-layouts  0.72 us (2%)
    pallas_call x1, Pallas kernels, channelize(): pl.pallas_call(functools.partial(channel_kernel, frames), out_shape=[jax....  39.3 us
    pallas_call x1, Pallas kernels, tile_sums(): pl.pallas_call(functools.partial(tile_kernel, scale), out_shape=jax.Shape...  2.6 us

profile of v3, /device:TPU:1, one launch (start us, length us, event | category | flops | bytes accessed | tf_op | source)
XLA Modules:
  0.0 42.6 jit_solution(10150143660575082887)
XLA Ops:
  0.0 0.0 copy-start
  0.0 0.7 %copy-done = f32[8,512]{1,0:T(8,128)S(1)} copy-done((f32[8,512]{1,0:T(8,128)S(1)}, f32[8,512]{1,0:T(8,128)}, u32[]{:S(2)}) %copy-start) | copy-done | bytes 16408
  0.7 39.3 %shard_map.37 = (bf16[1,1024,128]{2,1,0:T(8,128)(2,1)S(1)}, f32[6,2,128,128]{3,2,1,0:T(8,128)S(1)}, f32[6,2,128,128]{3,2,1,0:T(8,128)S(1)}, f32[6,2,128,128]{3,2...) custom-call(bf16[16,32768]{1,0:T(8,128)(2,1)} %v_hbm.1, ...), custom_call_target="tpu_custom_call" | custom-call | tf_op jit(solution)/shard_map/pallas_call | solution.py:299
  40.0 2.6 %shard_map.38 = f32[1,36,2,128,128]{4,3,2,1,0:T(8,128)} custom-call(bf16[1,1024,128]{2,1,0:T(8,128)(2,1)S(1)} %get-tuple-element.12.late, f32[6,2,128,128]{3,2,1,0:T(8,128)S(1)} %get-tuple-element.13.refs_0_, f32[6,2,128,128]{3,2,1,0:T(8,128)S(1)} %get-tuple-element.14.refs_1_, f32[6,2,128,128]{3,2,1,0:T(8,128)S(1)} %get-tuple-element.15.refs_2_, ...), custom_call_target="tpu_custom_call" | custom-call | tf_op jit(solution)/shard_map/pallas_call | solution.py:357
Async XLA Ops:
  0.0 0.7 %copy-start = (f32[8,512]{1,0:T(8,128)S(1)}, f32[8,512]{1,0:T(8,128)}, u32[]{:S(2)}) copy-start(f32[8,512]{1,0:T(8,128)} %taps_hbm.1) | copy-start | bytes 49156

commit v4 on v3

--- a/solution.py
+++ b/solution.py
@@ -18,8 +18,7 @@
 EARLY = 3
 PITCH = 136
 PARTS = 6
-TABLE_COPIES = 3
-VMEM_BYTES = 51298304
+VMEM_BYTES = 40 << 20
 MESH = pl.DeviceIdType.MESH
 
 
@@ -31,7 +30,7 @@
     vals = np.stack([np.cos(angle), -np.sin(angle)]) / length**0.5
     vals = vals.reshape(2, chans // owners, owners, length).transpose(2, 0, 1, 3)
     vals = vals.reshape(2 * chans, length).astype(np.float32).astype(jnp.bfloat16)
-    return np.concatenate([vals] * TABLE_COPIES)
+    return vals
 
 
 def grid_coords():
@@ -63,7 +62,7 @@
         part = pl.ds(c * chunk * FRAME, chunk * FRAME)
         load_volts.append(pltpu.make_async_copy(v_hbm.at[:, part], volts.at[:, part], in_sems.at[c]))
     load_taps = pltpu.make_async_copy(taps_hbm, taps_ref, in_sems.at[CHUNKS])
-    load_table = pltpu.make_async_copy(table_hbm.at[0 : 2 * F], table, in_sems.at[CHUNKS + 1])
+    load_table = pltpu.make_async_copy(table_hbm, table, in_sems.at[CHUNKS + 1])
     load_taps.start()
     for load in load_volts:
         load.start()
@@ -134,6 +133,17 @@
     for peer in x_peers:
         pl.semaphore_signal(x_sem, inc=1, device_id=peer, device_id_type=MESH)
 
+    def round_frames(low, high):
+        for pair in range(inp // 2):
+            for half in range(2):
+                to, src = (2 * pair + half) * frames, pair * PITCH + half * frames
+                for part in range(FRAME // LANES):
+                    filt[to + low : to + high, part * LANES : (part + 1) * LANES] = filt32[
+                        part, src + low : src + high, :
+                    ].astype(jnp.bfloat16)
+
+    round_frames(2 * TAPS, frames)
+
     @pl.when(block > 0)
     def _():
         halo_copy.wait_recv()
@@ -148,6 +158,7 @@
         return volts[:, d * FRAME + lane : d * FRAME + lane + LANES]
 
     filter_frames(0, read_first)
+    round_frames(0, 2 * TAPS)
     load_table.wait()
 
     low = lax.broadcasted_iota(jnp.int32, (8, LANES), 1) < LANES // 2
@@ -161,20 +172,6 @@
         rows = table[pl.ds(pl.multiple_of(owner * 2 * groups, 2 * groups), 2 * groups), :]
         for q in range(4):
             quarter = slice(q * 256, (q + 1) * 256)
-            if j == 0:
-                filt[quarter, :] = jnp.concatenate(
-                    [
-                        jnp.concatenate(
-                            [
-                                filt32[part, pair * PITCH : pair * PITCH + 2 * frames, :]
-                                for pair in (2 * q, 2 * q + 1)
-                            ],
-                            axis=0,
-                        )
-                        for part in range(FRAME // LANES)
-                    ],
-                    axis=1,
-                ).astype(jnp.bfloat16)
             spec = lax.dot_general(
                 rows,
                 filt[quarter, :],
@@ -370,7 +367,8 @@
 def on_device(voltages, pfb_taps):
     table = jnp.asarray(dft_table(F, FRAME, lax.axis_size("tm")))
     frames = voltages.shape[1] // FRAME
-    late, *sums = channelize(voltages, pfb_taps, table)
+    args = [pltpu.with_memory_space_constraint(a, pltpu.HBM) for a in (voltages, pfb_taps, table)]
+    late, *sums = channelize(*args)
     return tile_sums(late, sums, 1.0 / (frames * lax.axis_size("tm")))
 
 

time: 42.8 us -> 42 us (0.981)
  local copies, waits for them, and re-layouts: 0.72 us -> 0 us
    unnamed x2 -> x0, local copies, waits for them, and re-layouts: 0.72 us -> none
where the time goes in v4:
time: 42 us; the launch traced here: 41.9 us
  Pallas kernels  41.9 us (100%)
    pallas_call x1, Pallas kernels, channelize(): pl.pallas_call(functools.partial(channel_kernel, frames), out_shape=[jax....  39.3 us
    pallas_call x1, Pallas kernels, tile_sums(): pl.pallas_call(functools.partial(tile_kernel, scale), out_shape=jax.Shape...  2.6 us

profile of v4, /device:TPU:1, one launch (start us, length us, event | category | flops | bytes accessed | tf_op | source)
XLA Modules:
  0.0 41.9 jit_solution(30512609403939828)
XLA Ops:
  0.0 39.3 %shard_map.37 = (bf16[1,1024,128]{2,1,0:T(8,128)(2,1)S(1)}, f32[6,2,128,128]{3,2,1,0:T(8,128)S(1)}, f32[6,2,128,128]{3,2,1,0:T(8,128)S(1)}, f32[6,2,128,128]{3,2...) custom-call(bf16[16,32768]{1,0:T(8,128)(2,1)} %v_hbm.1, ...), custom_call_target="tpu_custom_call" | custom-call | tf_op jit(solution)/shard_map/pallas_call | solution.py:296
  39.3 2.6 %shard_map.38 = f32[1,36,2,128,128]{4,3,2,1,0:T(8,128)} custom-call(bf16[1,1024,128]{2,1,0:T(8,128)(2,1)S(1)} %get-tuple-element.12.late, f32[6,2,128,128]{3,2,1,0:T(8,128)S(1)} %get-tuple-element.13.refs_0_, f32[6,2,128,128]{3,2,1,0:T(8,128)S(1)} %get-tuple-element.14.refs_1_, f32[6,2,128,128]{3,2,1,0:T(8,128)S(1)} %get-tuple-element.15.refs_2_, ...), custom_call_target="tpu_custom_call" | custom-call | tf_op jit(solution)/shard_map/pallas_call | solution.py:354

commit v5 on v4

--- a/solution.py
+++ b/solution.py
@@ -14,7 +14,7 @@
 FRAME = 512
 HALO = (TAPS - 1) * FRAME
 LANES = 128
-CHUNKS = 8
+CHUNKS = 4
 EARLY = 3
 PITCH = 136
 PARTS = 6
@@ -63,10 +63,6 @@
         load_volts.append(pltpu.make_async_copy(v_hbm.at[:, part], volts.at[:, part], in_sems.at[c]))
     load_taps = pltpu.make_async_copy(taps_hbm, taps_ref, in_sems.at[CHUNKS])
     load_table = pltpu.make_async_copy(table_hbm, table, in_sems.at[CHUNKS + 1])
-    load_taps.start()
-    for load in load_volts:
-        load.start()
-
     barrier = pltpu.get_barrier_semaphore()
     z_peers = [grid_device(x_hi, y, lax.rem(z + d, 8), block) for d in range(1, 8)]
     y_peers = [grid_device(x_hi, lax.rem(y + d, 4), z, block) for d in range(1, 4)]
@@ -75,6 +71,9 @@
     ]
     for peer in x_peers + z_peers + y_peers:
         pl.semaphore_signal(barrier, inc=1, device_id=peer, device_id_type=MESH)
+    load_taps.start()
+    for load in load_volts:
+        load.start()
 
     load_table.start()
 

time: 42 us -> 41.8 us (level)
  no operation moved by 1% of the time
where the time goes in v5:
time: 41.8 us
  Pallas kernels  41.8 us (100%)
    pallas_call x1, Pallas kernels, channelize(): pl.pallas_call(functools.partial(channel_kernel, frames), out_shape=[jax....  39.2 us
    pallas_call x1, Pallas kernels, tile_sums(): pl.pallas_call(functools.partial(tile_kernel, scale), out_shape=jax.Shape...  2.6 us

profile of v5, /device:TPU:1, one launch (start us, length us, event | category | flops | bytes accessed | tf_op | source)
XLA Modules:
  0.0 41.8 jit_solution(14980791845821422435)
XLA Ops:
  0.0 39.2 %shard_map.37 = (bf16[1,1024,128]{2,1,0:T(8,128)(2,1)S(1)}, f32[6,2,128,128]{3,2,1,0:T(8,128)S(1)}, f32[6,2,128,128]{3,2,1,0:T(8,128)S(1)}, f32[6,2,128,128]{3,2...) custom-call(bf16[16,32768]{1,0:T(8,128)(2,1)} %v_hbm.1, ...), custom_call_target="tpu_custom_call" | custom-call | tf_op jit(solution)/shard_map/pallas_call | solution.py:295
  39.2 2.6 %shard_map.38 = f32[1,36,2,128,128]{4,3,2,1,0:T(8,128)} custom-call(bf16[1,1024,128]{2,1,0:T(8,128)(2,1)S(1)} %get-tuple-element.12.late, f32[6,2,128,128]{3,2,1,0:T(8,128)S(1)} %get-tuple-element.13.refs_0_, f32[6,2,128,128]{3,2,1,0:T(8,128)S(1)} %get-tuple-element.14.refs_1_, f32[6,2,128,128]{3,2,1,0:T(8,128)S(1)} %get-tuple-element.15.refs_2_, ...), custom_call_target="tpu_custom_call" | custom-call | tf_op jit(solution)/shard_map/pallas_call | solution.py:353

commit v6 on v5

--- a/solution.py
+++ b/solution.py
@@ -187,7 +187,7 @@
                     base = g * 8 * inp + pair
                     stage[pl.ds(base, 8, stride=inp), :] = first
                     stage[pl.ds(base + 8, 8, stride=inp), :] = second
-        send[j * span : (j + 1) * span, :] = stage[...].astype(jnp.bfloat16)
+        send[j * span : (j + 1) * span, :] = stage[0:span, :].astype(jnp.bfloat16)
 
     def copy_to(j, device, row):
         return pltpu.make_async_remote_copy(
@@ -307,9 +307,9 @@
             pltpu.VMEM((TAPS, FRAME), jnp.float32),
             pltpu.VMEM((2 * F, FRAME), jnp.bfloat16),
             pltpu.VMEM((inp, HALO), jnp.bfloat16),
-            pltpu.VMEM((FRAME // LANES, 8 * PITCH, LANES), jnp.float32),
+            pltpu.VMEM((FRAME // LANES, 8 * PITCH + 2 * frames, LANES), jnp.float32),
             pltpu.VMEM((rows, FRAME), jnp.bfloat16),
-            pltpu.VMEM((64 * inp, LANES), jnp.float32),
+            pltpu.VMEM((64 * inp + inp, LANES), jnp.float32),
             pltpu.VMEM((4 * 64 * inp, LANES), jnp.bfloat16),
             pltpu.VMEM((EARLY * 64 * inp, LANES), jnp.bfloat16),
             pltpu.SemaphoreType.DMA((CHUNKS + 2,)),

time: 41.8 us -> 41.8 us (level)
  no operation moved by 1% of the time
where the time goes in v6:
time: 41.8 us
  Pallas kernels  41.8 us (100%)
    pallas_call x1, Pallas kernels, channelize(): pl.pallas_call(functools.partial(channel_kernel, frames), out_shape=[jax....  39.2 us
    pallas_call x1, Pallas kernels, tile_sums(): pl.pallas_call(functools.partial(tile_kernel, scale), out_shape=jax.Shape...  2.6 us

profile of v6, /device:TPU:1, one launch (start us, length us, event | category | flops | bytes accessed | tf_op | source)
XLA Modules:
  0.0 41.8 jit_solution(3351294605053813374)
XLA Ops:
  0.0 39.2 %shard_map.37 = (bf16[1,1024,128]{2,1,0:T(8,128)(2,1)S(1)}, f32[6,2,128,128]{3,2,1,0:T(8,128)S(1)}, f32[6,2,128,128]{3,2,1,0:T(8,128)S(1)}, f32[6,2,128,128]{3,2...) custom-call(bf16[16,32768]{1,0:T(8,128)(2,1)} %v_hbm.1, ...), custom_call_target="tpu_custom_call" | custom-call | tf_op jit(solution)/shard_map/pallas_call | solution.py:295
  39.2 2.6 %shard_map.38 = f32[1,36,2,128,128]{4,3,2,1,0:T(8,128)} custom-call(bf16[1,1024,128]{2,1,0:T(8,128)(2,1)S(1)} %get-tuple-element.12.late, f32[6,2,128,128]{3,2,1,0:T(8,128)S(1)} %get-tuple-element.13.refs_0_, f32[6,2,128,128]{3,2,1,0:T(8,128)S(1)} %get-tuple-element.14.refs_1_, f32[6,2,128,128]{3,2,1,0:T(8,128)S(1)} %get-tuple-element.15.refs_2_, ...), custom_call_target="tpu_custom_call" | custom-call | tf_op jit(solution)/shard_map/pallas_call | solution.py:353

commit v7 on v6

--- a/solution.py
+++ b/solution.py
@@ -214,10 +214,11 @@
         transform(j)
         if j == 0:
             send_range(j, 1, groups // 2, 0)
-            pl.semaphore_wait(x_sem, len(x_peers))
-            send_range(j, groups // 2, groups, 0)
             early[pl.ds(slot, inp), :] = send[pl.ds(slot, inp), :]
         else:
+            if j == 1:
+                pl.semaphore_wait(x_sem, len(x_peers))
+                send_range(0, groups // 2, groups, 0)
             send_range(j, 0, groups, 1)
 
     @pl.when(block < blocks - 1)

time: 41.8 us -> 41.8 us (level)
  no operation moved by 1% of the time
where the time goes in v7:
time: 41.8 us
  Pallas kernels  41.7 us (100%)
    pallas_call x1, Pallas kernels, channelize(): pl.pallas_call(functools.partial(channel_kernel, frames), out_shape=[jax....  39.1 us
    pallas_call x1, Pallas kernels, tile_sums(): pl.pallas_call(functools.partial(tile_kernel, scale), out_shape=jax.Shape...  2.6 us

profile of v7, /device:TPU:1, one launch (start us, length us, event | category | flops | bytes accessed | tf_op | source)
XLA Modules:
  0.0 41.8 jit_solution(10837317465073299811)
XLA Ops:
  0.0 39.1 %shard_map.37 = (bf16[1,1024,128]{2,1,0:T(8,128)(2,1)S(1)}, f32[6,2,128,128]{3,2,1,0:T(8,128)S(1)}, f32[6,2,128,128]{3,2,1,0:T(8,128)S(1)}, f32[6,2,128,128]{3,2...) custom-call(bf16[16,32768]{1,0:T(8,128)(2,1)} %v_hbm.1, ...), custom_call_target="tpu_custom_call" | custom-call | tf_op jit(solution)/shard_map/pallas_call | solution.py:296
  39.2 2.6 %shard_map.38 = f32[1,36,2,128,128]{4,3,2,1,0:T(8,128)} custom-call(bf16[1,1024,128]{2,1,0:T(8,128)(2,1)S(1)} %get-tuple-element.12.late, f32[6,2,128,128]{3,2,1,0:T(8,128)S(1)} %get-tuple-element.13.refs_0_, f32[6,2,128,128]{3,2,1,0:T(8,128)S(1)} %get-tuple-element.14.refs_1_, f32[6,2,128,128]{3,2,1,0:T(8,128)S(1)} %get-tuple-element.15.refs_2_, ...), custom_call_target="tpu_custom_call" | custom-call | tf_op jit(solution)/shard_map/pallas_call | solution.py:354
